TPU v7x, 32 devices: a whole 2x2x4 slice. The times are simulated.
32 devices in a mesh: dp: 4 (over y, x), seq: 2 (over core), fsdp: 4 (over z).
Axes of the slice: x: 2, y: 2, z: 4, core: 2. Of those that a mesh axis runs over, the one named last changes fastest.
Arguments:
- signal: bfloat16 [16, 256, 1024], P(('dp', 'fsdp'), 'seq'), may hold values from -100 to 100
- w_query: bfloat16 [1024, 512], P('fsdp'), may hold values from -1 to 1
- w_key: bfloat16 [1024, 512], P('fsdp'), may hold values from -1 to 1
- w_value: bfloat16 [1024, 512], P('fsdp'), may hold values from -0.1875 to 0.1875
- w_output: bfloat16 [1024, 512], P('fsdp'), may hold values from -0.25 to 0.25
- upstream: bfloat16 [16, 256, 1024], P(('dp', 'fsdp'), 'seq'), may hold values from -6 to 6
Outputs:
- output: bfloat16 [16, 256, 1024], P(('dp', 'fsdp'), 'seq')
- grad_signal: bfloat16 [16, 256, 1024], P(('dp', 'fsdp'), 'seq')
- grad_query: float32 [1024, 512], P('fsdp')
- grad_key: float32 [1024, 512], P('fsdp')
- grad_value: float32 [1024, 512], P('fsdp')
- grad_output: float32 [1024, 512], P('fsdp')
All inputs are finite; a program needn't handle non-finite values.
Results may differ from a plain program's by a relative error of at most 0.02.
The roundings to bfloat16 on the way count: a program that leaves them out, or rounds other values in their place, can miss the bound.
Values may be sent and summed in bfloat16 or wider, within the bound.
A program may use at most 128 MiB of HBM per device.

v0:
```python
import jax
import jax.numpy as jnp
from jax import lax
from jax.sharding import PartitionSpec as P

HEADS = 8
HSIZE = 64


def normalize(frame_rows):
    widened = frame_rows.astype(jnp.float32)
    centre = widened - jnp.mean(widened, axis=-1, keepdims=True)
    variance = jnp.mean(centre * centre, axis=-1, keepdims=True)
    inverse = lax.rsqrt(variance + 1e-05)
    return (centre * inverse, inverse)


def split_heads(matrix):
    return matrix.reshape(matrix.shape[0], HEADS, HSIZE)


def dot_across(left, right):
    return lax.dot_general(
        left, right, (((0,), (0,)), ((), ())), preferred_element_type=jnp.float32
    )


def dot_against(left, right):
    return lax.dot_general(
        left, right, (((1,), (1,)), ((), ())), preferred_element_type=jnp.float32
    )


def body(signal, w_query, w_key, w_value, w_output, upstream):
    q_weight, k_weight, v_weight, o_weight = (
        lax.all_gather(w_query, "fsdp", axis=0, tiled=True),
        lax.all_gather(w_key, "fsdp", axis=0, tiled=True),
        lax.all_gather(w_value, "fsdp", axis=0, tiled=True),
        lax.all_gather(w_output, "fsdp", axis=0, tiled=True),
    )
    score_scale = HSIZE ** (-0.5)
    frame_rows = signal[0]
    grad_frames = upstream[0]
    local_frames = frame_rows.shape[0]
    width_heads = q_weight.shape[1]
    normed_f, inverse = normalize(frame_rows)
    normed = normed_f.astype(jnp.bfloat16)
    queries = jnp.dot(normed, q_weight, preferred_element_type=jnp.float32).astype(jnp.bfloat16)
    key_rows = jnp.dot(normed, k_weight, preferred_element_type=jnp.float32).astype(jnp.bfloat16)
    value_rows = jnp.dot(normed, v_weight, preferred_element_type=jnp.float32).astype(jnp.bfloat16)
    all_keys, all_values = (
        lax.all_gather(key_rows, "seq", axis=0, tiled=True),
        lax.all_gather(value_rows, "seq", axis=0, tiled=True),
    )
    query_heads = split_heads(queries)
    key_heads = split_heads(all_keys)
    value_heads = split_heads(all_values)
    scores = (
        jnp.einsum("qhs,khs->hqk", query_heads, key_heads, preferred_element_type=jnp.float32)
        * score_scale
    )
    row_max = jnp.max(scores, axis=-1, keepdims=True)
    exponent = jnp.exp(scores - row_max)
    row_total = jnp.sum(exponent, axis=-1, keepdims=True)
    attention = exponent / row_total
    attn_weights = attention.astype(jnp.bfloat16)
    context = jnp.einsum(
        "hqk,khs->qhs", attn_weights, value_heads, preferred_element_type=jnp.float32
    )
    context = context.reshape(local_frames, width_heads).astype(jnp.bfloat16)
    projected = dot_against(context, o_weight)
    output_rows = (frame_rows.astype(jnp.float32) + projected).astype(jnp.bfloat16)
    grad_context = jnp.dot(grad_frames, o_weight, preferred_element_type=jnp.float32).astype(
        jnp.bfloat16
    )
    grad_heads = split_heads(grad_context)
    grad_attention = jnp.einsum(
        "qhs,khs->hqk", grad_heads, value_heads, preferred_element_type=jnp.float32
    )
    row_delta = jnp.sum(attention * grad_attention, axis=-1, keepdims=True)
    grad_scores = (attention * (grad_attention - row_delta) * score_scale).astype(jnp.bfloat16)
    grad_queries = jnp.einsum(
        "hqk,khs->qhs", grad_scores, key_heads, preferred_element_type=jnp.float32
    )
    grad_queries = grad_queries.reshape(local_frames, width_heads).astype(jnp.bfloat16)
    all_queries, all_grad_context = (
        lax.all_gather(queries, "seq", axis=0, tiled=True),
        lax.all_gather(grad_context, "seq", axis=0, tiled=True),
    )
    all_max, all_total, all_delta = (
        lax.all_gather(row_max, "seq", axis=1, tiled=True),
        lax.all_gather(row_total, "seq", axis=1, tiled=True),
        lax.all_gather(row_delta, "seq", axis=1, tiled=True),
    )
    far_query_heads = split_heads(all_queries)
    far_grad_heads = split_heads(all_grad_context)
    own_keys = split_heads(key_rows)
    own_values = split_heads(value_rows)
    far_scores = (
        jnp.einsum("qhs,khs->hqk", far_query_heads, own_keys, preferred_element_type=jnp.float32)
        * score_scale
    )
    far_attention = jnp.exp(far_scores - all_max) / all_total
    far_weights = far_attention.astype(jnp.bfloat16)
    far_grad = jnp.einsum(
        "qhs,khs->hqk", far_grad_heads, own_values, preferred_element_type=jnp.float32
    )
    far_scaled = (far_attention * (far_grad - all_delta) * score_scale).astype(jnp.bfloat16)
    grad_keys = jnp.einsum(
        "hqk,qhs->khs", far_scaled, far_query_heads, preferred_element_type=jnp.float32
    )
    grad_keys = grad_keys.reshape(local_frames, width_heads).astype(jnp.bfloat16)
    grad_values = jnp.einsum(
        "hqk,qhs->khs", far_weights, far_grad_heads, preferred_element_type=jnp.float32
    )
    grad_values = grad_values.reshape(local_frames, width_heads).astype(jnp.bfloat16)
    grad_normed = (
        dot_against(grad_queries, q_weight)
        + dot_against(grad_keys, k_weight)
        + dot_against(grad_values, v_weight)
    )
    grad_mean = jnp.mean(grad_normed, axis=-1, keepdims=True)
    grad_along = jnp.mean(grad_normed * normed_f, axis=-1, keepdims=True)
    grad_rows = grad_frames.astype(jnp.float32) + inverse * (
        grad_normed - grad_mean - normed_f * grad_along
    )
    grad_rows = grad_rows.astype(jnp.bfloat16)
    shares = lax.psum_scatter(
        jnp.concatenate(
            [
                dot_across(normed, grad_queries),
                dot_across(normed, grad_keys),
                dot_across(normed, grad_values),
                dot_across(grad_frames, context),
            ],
            axis=1,
        ).astype(jnp.bfloat16),
        "fsdp",
        scatter_dimension=0,
        tiled=True,
    ).astype(jnp.float32)
    totals = lax.psum(shares, ("dp", "seq"))
    token_count = (
        signal.shape[0]
        * lax.axis_size("dp")
        * lax.axis_size("fsdp")
        * local_frames
        * lax.axis_size("seq")
    )
    totals = totals * token_count ** (-0.5)
    return (
        output_rows[None],
        grad_rows[None],
        totals[:, :width_heads],
        totals[:, width_heads : 2 * width_heads],
        totals[:, 2 * width_heads : 3 * width_heads],
        totals[:, 3 * width_heads :],
    )


def solution(mesh):
    placed = (
        P(("dp", "fsdp"), "seq", None),
        P("fsdp", None),
        P("fsdp", None),
        P("fsdp", None),
        P("fsdp", None),
        P(("dp", "fsdp"), "seq", None),
    )
    return jax.shard_map(
        body,
        mesh=mesh,
        in_specs=placed,
        out_specs=(
            P(("dp", "fsdp"), "seq", None),
            P(("dp", "fsdp"), "seq", None),
            P("fsdp", None),
            P("fsdp", None),
            P("fsdp", None),
            P("fsdp", None),
        ),
        check_vma=False,
    )
```

profile of v0, /device:TPU:1, one launch (start us, length us, event | category | flops | bytes accessed | tf_op | source)
XLA Modules:
  0.0 290.3 jit_solution(7552763304429266275)
XLA Ops:
  7.2 0.7 all-gather.14.cloned.1.call-update
  8.0 0.7 all-gather.8.cloned.1.call-update
  8.7 0.7 all-gather.12.cloned.1.call-update
  9.4 0.5 all-gather.10.cloned.1.call-update
  10.0 1.1 convert_reduce_fusion
  11.1 1.2 fusion.24
  12.3 27.2 %all-gather.14.cloned.1.call-done = bf16[1024,512]{1,0:T(8,128)(2,1)} async-done(((bf16[256,512]{1,0:T(8,128)(2,1)}), bf16[1024,512]{1,0:T(8,128)(2,1)}) %all-gather.14.cloned.1.call-update) | async-done | bytes 1048592 | tf_op jit(solution)/shard_map/all_gather | solution.py:39
  39.5 1.6 convolution_convert_fusion.7
  41.2 27.3 %all-gather.8.cloned.1.call-done = bf16[1024,512]{1,0:T(8,128)(2,1)} async-done(((bf16[256,512]{1,0:T(8,128)(2,1)}), bf16[1024,512]{1,0:T(8,128)(2,1)}) %all-gather.8.cloned.1.call-update) | async-done | bytes 1048592 | tf_op jit(solution)/shard_map/all_gather | solution.py:38
  68.5 1.7 convolution_convert_fusion.10
  70.3 27.2 %all-gather.12.cloned.1.call-done = bf16[1024,512]{1,0:T(8,128)(2,1)} async-done(((bf16[256,512]{1,0:T(8,128)(2,1)}), bf16[1024,512]{1,0:T(8,128)(2,1)}) %all-gather.12.cloned.1.call-update) | async-done | bytes 1048592 | tf_op jit(solution)/shard_map/all_gather | solution.py:37
  97.6 1.6 convolution_convert_fusion.8
  99.3 2.4 all_gather.42
  101.7 2.0 all_gather.34
  103.7 2.0 all_gather.37
  105.7 20.8 %all-gather.10.cloned.1.call-done = bf16[1024,512]{1,0:T(8,128)(2,1)} async-done(((bf16[256,512]{1,0:T(8,128)(2,1)}), bf16[1024,512]{1,0:T(8,128)(2,1)}) %all-gather.10.cloned.1.call-update) | async-done | bytes 1048592 | tf_op jit(solution)/shard_map/all_gather | solution.py:36
  126.4 1.6 convolution_convert_fusion.9
  128.1 2.4 all_gather.39
  130.7 0.1 copy.26
  131.1 0.4 fusion.49
  131.6 1.9 all-gather
  133.4 0.4 fusion.12
  133.8 1.8 all-gather.1
  135.6 1.2 convolution_convert_fusion.6
  136.8 0.8 multiply_reduce_fusion
  137.6 1.8 all-gather.2
  139.4 0.6 convolution_convert_fusion.5
  140.0 1.2 fusion.5
  141.2 0.2 convolution_convert_fusion.4
  141.5 0.5 convolution_convert_fusion
  142.1 0.7 fusion.10
  142.8 0.5 convolution_convert_fusion.1
  143.3 0.5 convolution_convert_fusion.2
  143.9 1.3 fusion
  145.2 2.3 pad_maximum_fusion
  147.6 2.6 fusion.9
  150.2 1.4 fusion.50
  151.6 0.5 convolution_add_fusion.1
  152.1 0.6 fusion.47
  152.7 1.0 fusion.34
  153.7 70.0 %reduce-scatter.2.cloned.1.call-done = bf16[256,2048]{0,1:T(8,128)(2,1)} async-done(((bf16[1024,2048]{0,1:T(8,128)(2,1)}), bf16[256,2048]{0,1:T(8,128)(2,1)}) %reduce-scatter.2.cloned.1.call-update) | async-done | bytes 1048592 | tf_op jit(solution)/shard_map/reduce_scatter | solution.py:128
  223.6 55.9 %all-reduce.1 = f32[256,2048]{0,1:T(8,128)S(1)} all-reduce(bf16[256,2048]{0,1:T(8,128)(2,1)} %reduce-scatter.2.cloned.1.call-done), channel_id=1, replica_groups=mesh['dp'=4,'seq'=2,'fsdp'=4] {'dp','seq'}, use_global_device_ids=true, to_apply=%region_8.0 | all-reduce | flops 524288 | bytes 3145728 | tf_op jit(solution)/shard_map/psum | solution.py:142
  279.5 0.1 broadcast_multiply_fusion
  279.7 0.1 fusion.48
  279.8 1.0 copy.37
  280.8 1.0 copy.36
  281.8 1.0 copy.35
  282.8 1.0 copy.34
  (34 shorter events, 1.3 us)
Async XLA Ops:
  7.2 90.4 %copy-start = (bf16[1,128,1024]{2,1,0:T(8,128)(2,1)S(1)}, bf16[1,128,1024]{2,1,0:T(8,128)(2,1)}, u32[]{:S(2)}) copy-start(bf16[1,128,1024]{2,1,0:T(8,128)(2,1)} %param.6) | copy-start | bytes 786436
  7.2 32.3 %all-gather.14.cloned.1.call-start = ((), (), s32[]{:S(2)}) async-start(), calls=%async_computation.4 | async-start | bytes 1310720 | tf_op jit(solution)/shard_map/all_gather | solution.py:39
  7.9 60.6 %all-gather.8.cloned.1.call-start = ((), (), s32[]{:S(2)}) async-start(), calls=%async_computation.1 | async-start | bytes 1310720 | tf_op jit(solution)/shard_map/all_gather | solution.py:38
  8.7 88.9 %all-gather.12.cloned.1.call-start = ((), (), s32[]{:S(2)}) async-start(), calls=%async_computation.3 | async-start | bytes 1310720 | tf_op jit(solution)/shard_map/all_gather | solution.py:37
  9.4 117.0 %all-gather.10.cloned.1.call-start = ((), (), s32[]{:S(2)}) async-start(), calls=%async_computation.2 | async-start | bytes 1310720 | tf_op jit(solution)/shard_map/all_gather | solution.py:36
  10.0 213.6 %reduce-scatter.2.cloned.1.call-start = ((), (), s32[]{:S(2)}) async-start(), calls=%async_computation.5 | async-start | bytes 5242880 | tf_op jit(solution)/shard_map/reduce_scatter | solution.py:128
  140.0 3.3 %copy-start.8 = (bf16[8,64,128]{2,1,0:T(8,128)(2,1)}, bf16[8,64,128]{2,1,0:T(8,128)(2,1)S(1)}, u32[]{:S(2)}) copy-start(bf16[8,64,128]{2,1,0:T(8,128)(2,1)S(1)} %convolution_convert_fusion.5) | copy-start | bytes 393220
  141.2 2.6 copy-start.4
  141.4 0.7 copy-start.6
  147.5 2.7 copy-start.3
  147.5 4.1 %copy-start.2 = (bf16[1024,512]{1,0:T(8,128)(2,1)S(1)}, bf16[1024,512]{1,0:T(8,128)(2,1)}, u32[]{:S(2)}) copy-start(bf16[1024,512]{1,0:T(8,128)(2,1)} %all-gather.12.cloned.1.call-done) | copy-start | bytes 3145732
  147.5 4.6 %copy-start.1 = (bf16[1024,512]{1,0:T(8,128)(2,1)S(1)}, bf16[1024,512]{1,0:T(8,128)(2,1)}, u32[]{:S(2)}) copy-start(bf16[1024,512]{1,0:T(8,128)(2,1)} %all-gather.8.cloned.1.call-done) | copy-start | bytes 3145732
  147.5 4.5 %copy-start.7 = (bf16[8,64,128]{2,1,0:T(8,128)(2,1)S(1)}, bf16[8,64,128]{2,1,0:T(8,128)(2,1)}, u32[]{:S(2)}) copy-start(bf16[8,64,128]{2,1,0:T(8,128)(2,1)} %copy-done.6) | copy-start | bytes 393220
  147.5 5.1 %copy-start.5 = (bf16[1,128,1024]{2,1,0:T(8,128)(2,1)S(1)}, bf16[1,128,1024]{2,1,0:T(8,128)(2,1)}, u32[]{:S(2)}) copy-start(bf16[1,128,1024]{2,1,0:T(8,128)(2,1)} %param.11) | copy-start | bytes 786436
Sparse Core Ops, SparseCore 0:
  9.6 29.8 all-gather.13
  41.1 27.4 all-gather.7
  70.1 27.4 all-gather.11
  99.0 27.4 all-gather.9
  147.7 75.9 reduce-scatter.1
where the time goes:
time: 293 us; the launch traced here: 290 us
  waiting for transfers between devices  175 us (60%)
  blocking collectives  70.2 us (24%)
  matrix products  19.5 us (7%)
  between operations  14.1 us (5%)
  other arithmetic  6.06 us (2%)
  local copies, waits for them, and re-layouts  5.28 us (2%)
    reduce_scatter x1, waiting for transfers between devices, body(): lax.psum_scatter(jnp.concatenate([dot_across(normed, grad_queries), dot_a...  70 us
    psum x1, blocking collectives, body(): totals = lax.psum(shares, ('dp', 'seq'))  55.9 us
    all_gather x1, waiting for transfers between devices, body(): lax.all_gather(w_value, 'fsdp', axis=0, tiled=True)  27.3 us
    all_gather x1, waiting for transfers between devices, body(): lax.all_gather(w_key, 'fsdp', axis=0, tiled=True)  27.2 us
    all_gather x1, waiting for transfers between devices, body(): lax.all_gather(w_output, 'fsdp', axis=0, tiled=True)  27.2 us
    all_gather x1, waiting for transfers between devices, body(): lax.all_gather(w_query, 'fsdp', axis=0, tiled=True)  20.8 us
  transfers between devices with their start and end apart: 5, of which 5 were waited for; matrix products, arithmetic and copies ran while one was open for 5% of the time, Pallas kernels for 0%

commit v1 on v0

--- a/solution.py
+++ b/solution.py
@@ -1,6 +1,8 @@
 import jax
 import jax.numpy as jnp
 from jax import lax
+from jax.experimental import pallas as pl
+from jax.experimental.pallas import tpu as pltpu
 from jax.sharding import PartitionSpec as P
 
 HEADS = 8
@@ -158,6 +160,246 @@
     )
 
 
+F32 = jnp.float32
+BF16 = jnp.bfloat16
+MESH = pl.DeviceIdType.MESH
+N_SEMS = 38
+
+
+def rows_of(index, size):
+    return pl.ds(pl.multiple_of(index * size, size), size)
+
+
+def fused_kernel(
+    token_count,
+    sig_ref, up_ref, wq_ref, wk_ref, wv_ref, wo_ref,
+    out_ref, gsig_ref, gq_ref, gk_ref, gv_ref, go_ref,
+    weights, sig_all, up_all, normed, qkv, gctx, ctx, grads3,
+    partial, landed, summed, landed_z, final,
+    out_send, out_recv, gn_send, gn_recv, send_sems, recv_sems,
+):
+    dp, core, z = lax.axis_index("dp"), lax.axis_index("seq"), lax.axis_index("fsdp")
+    n_dp, n_z = lax.axis_size("dp"), lax.axis_size("fsdp")
+    half = wq_ref.shape[1] // 2
+    block = wq_ref.shape[0]
+    piece = block // n_dp
+    frames = sig_ref.shape[0]
+    scale = HSIZE ** (-0.5)
+
+    def copy(src, dst, sem, axis, to):
+        return pltpu.make_async_remote_copy(
+            src_ref=src, dst_ref=dst, send_sem=send_sems.at[sem], recv_sem=recv_sems.at[sem],
+            device_id={axis: to}, device_id_type=MESH,
+        )
+
+    def forth(index, step, size):
+        return lax.rem(index + step, size)
+
+    def back(index, step, size):
+        return lax.rem(index + size - step, size)
+
+    barrier = pltpu.get_barrier_semaphore()
+    for step in range(1, n_dp):
+        pl.semaphore_signal(barrier, inc=1, device_id={"dp": forth(dp, step, n_dp)}, device_id_type=MESH)
+    for step in range(1, n_z):
+        pl.semaphore_signal(barrier, inc=1, device_id={"fsdp": forth(z, step, n_z)}, device_id_type=MESH)
+    pl.semaphore_signal(barrier, inc=1, device_id={"seq": 1 - core}, device_id_type=MESH)
+
+    own_cols = pl.ds(pl.multiple_of(core * half, half), half)
+    own_block = rows_of(z, block)
+    for at, ref in enumerate((wq_ref, wk_ref, wv_ref, wo_ref)):
+        weights[own_block, at * half : (at + 1) * half] = ref[:, own_cols]
+    pl.semaphore_wait(barrier, n_dp + n_z - 1)
+
+    sends = []
+
+    def start(*args):
+        one = copy(*args)
+        one.start()
+        sends.append(one)
+
+    def arrived(dst, sem):
+        copy(dst, dst, sem, "seq", 1 - core).wait_recv()
+
+    def weight_rows(shard, quarter):
+        return weights.at[pl.ds(pl.multiple_of(shard * block + quarter * piece, piece), piece)]
+
+    mine = weight_rows(z, dp)
+    for step in (1, 2, 3):
+        start(mine, mine, step - 1, "fsdp", forth(z, step, n_z))
+    own_frames = rows_of(core, frames)
+    far_frames = rows_of(1 - core, frames)
+    start(sig_ref, sig_all.at[own_frames], 12, "seq", 1 - core)
+    start(up_ref, up_all.at[own_frames], 13, "seq", 1 - core)
+    normed_f, inverse = normalize(sig_ref[...])
+    normed[own_frames, :] = normed_f.astype(BF16)
+    up_all[own_frames, :] = up_ref[...]
+    arrived(sig_all.at[far_frames], 12)
+    far_normed, _ = normalize(sig_all[far_frames, :])
+    normed[far_frames, :] = far_normed.astype(BF16)
+    arrived(up_all.at[far_frames], 13)
+
+    for step in (1, 2, 3):
+        source = back(z, step, n_z)
+        held = weight_rows(source, dp)
+        arrived(held, step - 1)
+        for peer in (1, 2, 3):
+            start(held, held, 3 + (step - 1) * 3 + peer - 1, "dp", forth(dp, peer, n_dp))
+
+    for step in (0, 1, 2, 3):
+        source = back(z, step, n_z)
+        if step:
+            for peer in (1, 2, 3):
+                arrived(weight_rows(source, back(dp, peer, n_dp)), 3 + (step - 1) * 3 + peer - 1)
+        rows = rows_of(source, block)
+        first = jnp.dot(normed[:, rows], weights[rows, : 3 * half], preferred_element_type=F32)
+        second = jnp.dot(up_all[:, rows], weights[rows, 3 * half :], preferred_element_type=F32)
+        if step:
+            first = qkv[...] + first
+            second = gctx[...] + second
+        qkv[...] = first
+        gctx[...] = second
+
+    for head in range(half // HSIZE):
+        cols = slice(head * HSIZE, (head + 1) * HSIZE)
+        query = qkv[:, head * HSIZE : (head + 1) * HSIZE].astype(BF16)
+        key = qkv[:, half + head * HSIZE : half + (head + 1) * HSIZE].astype(BF16)
+        value = qkv[:, 2 * half + head * HSIZE : 2 * half + (head + 1) * HSIZE].astype(BF16)
+        grad = gctx[:, cols].astype(BF16)
+        scores = dot_against(query, key) * scale
+        exponent = jnp.exp(scores - jnp.max(scores, axis=-1, keepdims=True))
+        attention = exponent / jnp.sum(exponent, axis=-1, keepdims=True)
+        attn_weights = attention.astype(BF16)
+        ctx[:, cols] = jnp.dot(attn_weights, value, preferred_element_type=F32).astype(BF16)
+        grad_attention = dot_against(grad, value)
+        delta = jnp.sum(attention * grad_attention, axis=-1, keepdims=True)
+        grad_scores = (attention * (grad_attention - delta) * scale).astype(BF16)
+        grads3[:, cols] = jnp.dot(grad_scores, key, preferred_element_type=F32).astype(BF16)
+        grads3[:, half + head * HSIZE : half + (head + 1) * HSIZE] = dot_across(
+            grad_scores, query
+        ).astype(BF16)
+        grads3[:, 2 * half + head * HSIZE : 2 * half + (head + 1) * HSIZE] = dot_across(
+            attn_weights, grad
+        ).astype(BF16)
+
+    order = (2, 1, 3, 0)
+    for step in order:
+        cols = rows_of(forth(z, step, n_z), block)
+        partial[step, :, : 3 * half] = dot_across(normed[:, cols], grads3[...]).astype(BF16)
+        partial[step, :, 3 * half :] = dot_across(up_all[:, cols], ctx[...]).astype(BF16)
+        for peer in (1, 2, 3):
+            to = forth(dp, peer, n_dp)
+            start(
+                partial.at[step, rows_of(to, piece)], landed.at[step, peer - 1],
+                14 + step * 3 + peer - 1, "dp", to,
+            )
+
+    out_send[...] = dot_against(ctx[far_frames, :], weights[:, 3 * half :])
+    start(out_send, out_recv, 26, "seq", 1 - core)
+    gn_send[...] = dot_against(grads3[far_frames, :], weights[:, : 3 * half])
+    start(gn_send, gn_recv, 27, "seq", 1 - core)
+    out_own = dot_against(ctx[own_frames, :], weights[:, 3 * half :])
+    arrived(out_recv, 26)
+    out_ref[...] = (sig_ref[...].astype(F32) + (out_own + out_recv[...])).astype(BF16)
+
+    for step in order:
+        for peer in (1, 2, 3):
+            arrived(landed.at[step, peer - 1], 14 + step * 3 + peer - 1)
+        total = partial[step, rows_of(dp, piece), :].astype(F32)
+        for peer in (1, 2, 3):
+            total = total + landed[step, peer - 1].astype(F32)
+        summed[step] = total.astype(BF16)
+        if step:
+            start(summed.at[step], landed_z.at[step - 1], 28 + step - 1, "fsdp", forth(z, step, n_z))
+
+    gn_own = dot_against(grads3[own_frames, :], weights[:, : 3 * half])
+    arrived(gn_recv, 27)
+    grad_normed = gn_own + gn_recv[...]
+    normed_f, inverse = normalize(sig_ref[...])
+    grad_mean = jnp.mean(grad_normed, axis=-1, keepdims=True)
+    grad_along = jnp.mean(grad_normed * normed_f, axis=-1, keepdims=True)
+    gsig_ref[...] = (
+        up_ref[...].astype(F32) + inverse * (grad_normed - grad_mean - normed_f * grad_along)
+    ).astype(BF16)
+
+    total = summed[0].astype(F32)
+    for step in (1, 2, 3):
+        arrived(landed_z.at[step - 1], 28 + step - 1)
+        total = total + landed_z[step - 1].astype(F32)
+    own_piece = rows_of(dp, piece)
+    final[core, own_piece, :] = total.astype(BF16)
+    place = final.at[core, own_piece]
+    for peer in (1, 2, 3):
+        start(place, place, 31 + peer - 1, "dp", forth(dp, peer, n_dp))
+    start(place, place, 34, "seq", 1 - core)
+    for peer in (1, 2, 3):
+        place = final.at[core, rows_of(back(dp, peer, n_dp), piece)]
+        arrived(place, 31 + peer - 1)
+        start(place, place, 34 + peer, "seq", 1 - core)
+    for peer in (0, 1, 2, 3):
+        arrived(final.at[1 - core, rows_of(back(dp, peer, n_dp), piece)], 34 + peer)
+
+    factor = token_count ** (-0.5)
+    for at, ref in enumerate((gq_ref, gk_ref, gv_ref, go_ref)):
+        for side in (0, 1):
+            ref[:, side * half : (side + 1) * half] = (
+                final[side, :, at * half : (at + 1) * half].astype(F32) * factor
+            )
+    for one in sends:
+        one.wait_send()
+
+
+def fused_body(signal, w_query, w_key, w_value, w_output, upstream):
+    frames, width = signal.shape[1:]
+    block, heads_width = w_query.shape
+    both, half = 2 * frames, heads_width // 2
+    n_dp, n_z = lax.axis_size("dp"), lax.axis_size("fsdp")
+    piece = block // n_dp
+    token_count = signal.shape[0] * n_dp * n_z * both
+    vmem = pl.BlockSpec(memory_space=pltpu.VMEM)
+    rows_shape = jax.ShapeDtypeStruct((frames, width), BF16)
+    grad_shape = jax.ShapeDtypeStruct((block, heads_width), F32)
+
+    def kernel(*refs):
+        fused_kernel(token_count, *refs)
+
+    output_rows, grad_rows, *grads = pl.pallas_call(
+        kernel,
+        out_shape=[rows_shape, rows_shape] + [grad_shape] * 4,
+        in_specs=[vmem] * 6,
+        out_specs=[vmem] * 6,
+        scratch_shapes=[
+            pltpu.VMEM((width, 4 * half), BF16),
+            pltpu.VMEM((both, width), BF16),
+            pltpu.VMEM((both, width), BF16),
+            pltpu.VMEM((both, width), BF16),
+            pltpu.VMEM((both, 3 * half), F32),
+            pltpu.VMEM((both, half), F32),
+            pltpu.VMEM((both, half), BF16),
+            pltpu.VMEM((both, 3 * half), BF16),
+            pltpu.VMEM((n_z, block, 4 * half), BF16),
+            pltpu.VMEM((n_z, n_dp - 1, piece, 4 * half), BF16),
+            pltpu.VMEM((n_z, piece, 4 * half), BF16),
+            pltpu.VMEM((n_z - 1, piece, 4 * half), BF16),
+            pltpu.VMEM((2, block, 4 * half), BF16),
+            pltpu.VMEM((frames, width), F32),
+            pltpu.VMEM((frames, width), F32),
+            pltpu.VMEM((frames, width), F32),
+            pltpu.VMEM((frames, width), F32),
+            pltpu.SemaphoreType.DMA((N_SEMS,)),
+            pltpu.SemaphoreType.DMA((N_SEMS,)),
+        ],
+        compiler_params=pltpu.CompilerParams(
+            collective_id=0, has_side_effects=True, vmem_limit_bytes=44 * 1024 * 1024
+        ),
+    )(signal[0], upstream[0], w_query, w_key, w_value, w_output)
+    return (output_rows[None], grad_rows[None], *grads)
+
+
+def fits(mesh):
+    return mesh.shape["dp"] == 4 and mesh.shape["seq"] == 2 and mesh.shape["fsdp"] == 4
+
+
 def solution(mesh):
     placed = (
         P(("dp", "fsdp"), "seq", None),
@@ -168,7 +410,7 @@
         P(("dp", "fsdp"), "seq", None),
     )
     return jax.shard_map(
-        body,
+        fused_body if fits(mesh) else body,
         mesh=mesh,
         in_specs=placed,
         out_specs=(

time: 293 us -> 75.3 us (0.26)
  waiting for transfers between devices: 175 us -> 0 us
  blocking collectives: 70.2 us -> 0 us
  Pallas kernels: 0 us -> 64.1 us
  matrix products: 19.5 us -> 0 us
  between operations: 14.1 us -> 0.66 us
  other arithmetic: 6.06 us -> 0 us
  local copies, waits for them, and re-layouts: 5.28 us -> 10.3 us
    all_gather x4 -> x0, waiting for transfers between devices: 102 us -> none  [the longest x1 27.3 us: body(): lax.all_gather(w_value, 'fsdp', axis=0, tiled=True)]
    reduce_scatter x1 -> x0, waiting for transfers between devices: 70 us -> none  [body(): lax.psum_scatter(jnp.concatenate([dot_across(normed, grad_queries), dot_a...]
    pallas_call x0 -> x1, Pallas kernels: none -> 64.1 us  [fused_body(): pl.pallas_call(kernel, out_shape=[rows_shape, rows_shape] + [grad_shape]...]
    psum x1 -> x0, blocking collectives: 55.9 us -> none  [body(): totals = lax.psum(shares, ('dp', 'seq'))]
    dot_general x19 -> x0, matrix products: 19.5 us -> none  [the longest x4 5.04 us: dot_against(): lax.dot_general(left, right, (((1,), (1,)), ((), ())), preferred_element_...]
    all_gather x7 -> x0, blocking collectives: 14.3 us -> none  [the longest x1 2.45 us: body(): lax.all_gather(grad_context, 'seq', axis=0, tiled=True)]
    unnamed x22 -> x18, local copies, waits for them, and re-layouts: 4.14 us -> 10.3 us
  transfers between devices with their start and end apart: 5 -> 0, of which waited for: 5 -> 0; matrix products, arithmetic and copies ran while one was open for 5% -> 0% of each run, Pallas kernels for 0% -> 0%
where the time goes in v1:
time: 75.3 us; the launch traced here: 75 us
  Pallas kernels  64.1 us (85%)
  local copies, waits for them, and re-layouts  10.3 us (14%)
    pallas_call x1, Pallas kernels, fused_body(): pl.pallas_call(kernel, out_shape=[rows_shape, rows_shape] + [grad_shape]...  64.1 us
    unnamed x18, local copies, waits for them, and re-layouts  10.3 us

profile of v1, /device:TPU:1, one launch (start us, length us, event | category | flops | bytes accessed | tf_op | source)
XLA Modules:
  0.0 75.0 jit_solution(18280897872477372670)
XLA Ops:
  0.6 0.0 copy-start
  0.6 0.9 %copy-done = bf16[1,128,1024]{2,1,0:T(8,128)(2,1)S(1)} copy-done((bf16[1,128,1024]{2,1,0:T(8,128)(2,1)S(1)}, bf16[1,128,1024]{2,1,0:T(8,128)(2,1)}, u32[]{:S(2)}) %copy-start) | copy-done | bytes 262168
  1.6 0.0 copy-start.1
  1.6 0.9 %copy-done.1 = bf16[1,128,1024]{2,1,0:T(8,128)(2,1)S(1)} copy-done((bf16[1,128,1024]{2,1,0:T(8,128)(2,1)S(1)}, bf16[1,128,1024]{2,1,0:T(8,128)(2,1)}, u32[]{:S(2)}) %copy-start.1) | copy-done | bytes 262168
  2.5 0.0 copy-start.2
  2.5 0.9 %copy-done.2 = bf16[256,512]{1,0:T(8,128)(2,1)S(1)} copy-done((bf16[256,512]{1,0:T(8,128)(2,1)S(1)}, bf16[256,512]{1,0:T(8,128)(2,1)}, u32[]{:S(2)}) %copy-start.2) | copy-done | bytes 262168
  3.5 0.0 copy-start.3
  3.5 0.9 %copy-done.3 = bf16[256,512]{1,0:T(8,128)(2,1)S(1)} copy-done((bf16[256,512]{1,0:T(8,128)(2,1)S(1)}, bf16[256,512]{1,0:T(8,128)(2,1)}, u32[]{:S(2)}) %copy-start.3) | copy-done | bytes 262168
  4.4 0.0 copy-start.4
  4.4 0.9 %copy-done.4 = bf16[256,512]{1,0:T(8,128)(2,1)S(1)} copy-done((bf16[256,512]{1,0:T(8,128)(2,1)S(1)}, bf16[256,512]{1,0:T(8,128)(2,1)}, u32[]{:S(2)}) %copy-start.4) | copy-done | bytes 262168
  5.4 0.0 copy-start.5
  5.4 0.9 %copy-done.5 = bf16[256,512]{1,0:T(8,128)(2,1)S(1)} copy-done((bf16[256,512]{1,0:T(8,128)(2,1)S(1)}, bf16[256,512]{1,0:T(8,128)(2,1)}, u32[]{:S(2)}) %copy-start.5) | copy-done | bytes 262168
  6.3 64.1 %shard_map.109 = (bf16[128,1024]{1,0:T(8,128)(2,1)S(1)}, bf16[128,1024]{1,0:T(8,128)(2,1)S(1)}, f32[256,512]{1,0:T(8,128)S(1)}, f32[256,512]{1,0:T(8,128)S(1)}, ...) custom-call(bf16[128,1024]{1,0:T(8,128)(2,1)S(1)} %bitcast.6, bf16[128,1024]{1,0:T(8,128)(2,1)S(1)} %bitcast.7, ...), custom_call_target="tpu_custom_call" | custom-call | tf_op jit(solution)/shard_map/pallas_call | solution.py:366
  70.4 0.7 copy.18
  71.1 0.7 copy.19
  71.8 0.8 %copy.20 = f32[256,512]{1,0:T(8,128)} copy(f32[256,512]{1,0:T(8,128)S(1)} %get-tuple-element.26) | data formatting | bytes 1048576
  72.6 0.8 %copy.21 = f32[256,512]{1,0:T(8,128)} copy(f32[256,512]{1,0:T(8,128)S(1)} %get-tuple-element.27) | data formatting | bytes 1048576
  73.4 0.8 %copy.22 = f32[256,512]{1,0:T(8,128)} copy(f32[256,512]{1,0:T(8,128)S(1)} %get-tuple-element.28) | data formatting | bytes 1048576
  74.2 0.8 %copy.23 = f32[256,512]{1,0:T(8,128)} copy(f32[256,512]{1,0:T(8,128)S(1)} %get-tuple-element.29) | data formatting | bytes 1048576
Async XLA Ops:
  0.6 1.0 %copy-start = (bf16[1,128,1024]{2,1,0:T(8,128)(2,1)S(1)}, bf16[1,128,1024]{2,1,0:T(8,128)(2,1)}, u32[]{:S(2)}) copy-start(bf16[1,128,1024]{2,1,0:T(8,128)(2,1)} %param.6) | copy-start | bytes 786436
  1.6 0.9 %copy-start.1 = (bf16[1,128,1024]{2,1,0:T(8,128)(2,1)S(1)}, bf16[1,128,1024]{2,1,0:T(8,128)(2,1)}, u32[]{:S(2)}) copy-start(bf16[1,128,1024]{2,1,0:T(8,128)(2,1)} %param.11) | copy-start | bytes 786436
  2.5 0.9 %copy-start.2 = (bf16[256,512]{1,0:T(8,128)(2,1)S(1)}, bf16[256,512]{1,0:T(8,128)(2,1)}, u32[]{:S(2)}) copy-start(bf16[256,512]{1,0:T(8,128)(2,1)} %refs_2_.1) | copy-start | bytes 786436
  3.5 0.9 %copy-start.3 = (bf16[256,512]{1,0:T(8,128)(2,1)S(1)}, bf16[256,512]{1,0:T(8,128)(2,1)}, u32[]{:S(2)}) copy-start(bf16[256,512]{1,0:T(8,128)(2,1)} %refs_3_.1) | copy-start | bytes 786436
  4.4 0.9 %copy-start.4 = (bf16[256,512]{1,0:T(8,128)(2,1)S(1)}, bf16[256,512]{1,0:T(8,128)(2,1)}, u32[]{:S(2)}) copy-start(bf16[256,512]{1,0:T(8,128)(2,1)} %refs_4_.1) | copy-start | bytes 786436
  5.4 0.9 %copy-start.5 = (bf16[256,512]{1,0:T(8,128)(2,1)S(1)}, bf16[256,512]{1,0:T(8,128)(2,1)}, u32[]{:S(2)}) copy-start(bf16[256,512]{1,0:T(8,128)(2,1)} %refs_5_.1) | copy-start | bytes 786436

commit v2 on v1

--- a/solution.py
+++ b/solution.py
@@ -172,18 +172,19 @@
 
 def fused_kernel(
     token_count,
-    sig_ref, up_ref, wq_ref, wk_ref, wv_ref, wo_ref,
+    rows_ref, w_ref,
     out_ref, gsig_ref, gq_ref, gk_ref, gv_ref, go_ref,
     weights, sig_all, up_all, normed, qkv, gctx, ctx, grads3,
     partial, landed, summed, landed_z, final,
     out_send, out_recv, gn_send, gn_recv, send_sems, recv_sems,
 ):
+    block, frames = w_ref.shape[0] // 4, rows_ref.shape[0] // 2
+    sig_ref, up_ref = (rows_ref.at[at * frames : (at + 1) * frames] for at in range(2))
+    wq_ref, wk_ref, wv_ref, wo_ref = (w_ref.at[at * block : (at + 1) * block] for at in range(4))
     dp, core, z = lax.axis_index("dp"), lax.axis_index("seq"), lax.axis_index("fsdp")
     n_dp, n_z = lax.axis_size("dp"), lax.axis_size("fsdp")
     half = wq_ref.shape[1] // 2
-    block = wq_ref.shape[0]
     piece = block // n_dp
-    frames = sig_ref.shape[0]
     scale = HSIZE ** (-0.5)
 
     def copy(src, dst, sem, axis, to):
@@ -366,7 +367,7 @@
     output_rows, grad_rows, *grads = pl.pallas_call(
         kernel,
         out_shape=[rows_shape, rows_shape] + [grad_shape] * 4,
-        in_specs=[vmem] * 6,
+        in_specs=[vmem] * 2,
         out_specs=[vmem] * 6,
         scratch_shapes=[
             pltpu.VMEM((width, 4 * half), BF16),
@@ -392,7 +393,10 @@
         compiler_params=pltpu.CompilerParams(
             collective_id=0, has_side_effects=True, vmem_limit_bytes=44 * 1024 * 1024
         ),
-    )(signal[0], upstream[0], w_query, w_key, w_value, w_output)
+    )(
+        jnp.concatenate([signal[0], upstream[0]], axis=0),
+        jnp.concatenate([w_query, w_key, w_value, w_output], axis=0),
+    )
     return (output_rows[None], grad_rows[None], *grads)
 
 

time: 75.3 us -> 71.1 us (0.944)
  local copies, waits for them, and re-layouts: 10.3 us -> 4.73 us
  other arithmetic: 0 us -> 1.21 us
    unnamed x18 -> x14, local copies, waits for them, and re-layouts: 10.3 us -> 4.73 us
    concatenate x0 -> x2, other arithmetic: none -> 1.21 us  [the longest x1 1.15 us: fused_body(): jnp.concatenate([signal[0], upstream[0]], axis=0)]
where the time goes in v2:
time: 71.1 us; the launch traced here: 70.9 us
  Pallas kernels  64.3 us (90%)
  local copies, waits for them, and re-layouts  4.73 us (7%)
  other arithmetic  1.21 us (2%)
    pallas_call x1, Pallas kernels, fused_body(): pl.pallas_call(kernel, out_shape=[rows_shape, rows_shape] + [grad_shape]...  64.3 us
    unnamed x14, local copies, waits for them, and re-layouts  4.73 us

profile of v2, /device:TPU:1, one launch (start us, length us, event | category | flops | bytes accessed | tf_op | source)
XLA Modules:
  0.0 70.9 jit_solution(4799253147336846807)
XLA Ops:
  0.6 0.0 copy-start
  0.6 0.0 copy-start.1
  0.7 0.0 copy-start.2
  0.7 0.0 copy-start.3
  0.7 1.1 %pad_maximum_fusion.1.refs_0_ = bf16[256,1024]{1,0:T(8,128)(2,1)S(1)} fusion(bf16[128,1024]{1,0:T(8,128)(2,1)} %bitcast.6, bf16[128,1024]{1,0:T(8,128)(2,1)} %bitcast.7), kind=kLoop, calls=%fused_computation.1 | loop fusion | flops 1048576 | bytes 1048576 | tf_op jit(solution)/shard_map/concatenate | solution.py:397
  1.8 0.0 copy-done
  1.8 0.0 copy-done.1
  1.8 0.1 copy-done.2
  1.9 0.1 copy-done.3
  2.0 0.1 pad_maximum_fusion.refs_1_
  2.1 64.3 %shard_map.109 = (bf16[128,1024]{1,0:T(8,128)(2,1)S(1)}, bf16[128,1024]{1,0:T(8,128)(2,1)S(1)}, f32[256,512]{1,0:T(8,128)S(1)}, f32[256,512]{1,0:T(8,128)S(1)}, ...) custom-call(bf16[256,1024]{1,0:T(8,128)(2,1)S(1)} %pad_maximum_fusion.1.refs_0_, bf16[1024,512]{1,0:T(8,128)(2,1)S(1)} %pad_maximum_fusion.refs_1_), custom_call_target="tpu_custom_call" | custom-call | tf_op jit(solution)/shard_map/pallas_call | solution.py:367
  66.3 0.7 copy.18
  67.1 0.7 copy.19
  67.8 0.8 %copy.20 = f32[256,512]{1,0:T(8,128)} copy(f32[256,512]{1,0:T(8,128)S(1)} %get-tuple-element.26) | data formatting | bytes 1048576
  68.5 0.8 %copy.21 = f32[256,512]{1,0:T(8,128)} copy(f32[256,512]{1,0:T(8,128)S(1)} %get-tuple-element.27) | data formatting | bytes 1048576
  69.3 0.8 %copy.22 = f32[256,512]{1,0:T(8,128)} copy(f32[256,512]{1,0:T(8,128)S(1)} %get-tuple-element.28) | data formatting | bytes 1048576
  70.1 0.8 %copy.23 = f32[256,512]{1,0:T(8,128)} copy(f32[256,512]{1,0:T(8,128)S(1)} %get-tuple-element.29) | data formatting | bytes 1048576
Async XLA Ops:
  0.6 1.2 %copy-start = (bf16[256,512]{1,0:T(8,128)(2,1)S(1)}, bf16[256,512]{1,0:T(8,128)(2,1)}, u32[]{:S(2)}) copy-start(bf16[256,512]{1,0:T(8,128)(2,1)} %param.10) | copy-start | bytes 786436
  0.6 1.2 %copy-start.1 = (bf16[256,512]{1,0:T(8,128)(2,1)S(1)}, bf16[256,512]{1,0:T(8,128)(2,1)}, u32[]{:S(2)}) copy-start(bf16[256,512]{1,0:T(8,128)(2,1)} %param.9) | copy-start | bytes 786436
  0.7 1.2 %copy-start.2 = (bf16[256,512]{1,0:T(8,128)(2,1)S(1)}, bf16[256,512]{1,0:T(8,128)(2,1)}, u32[]{:S(2)}) copy-start(bf16[256,512]{1,0:T(8,128)(2,1)} %param.8) | copy-start | bytes 786436
  0.7 1.3 %copy-start.3 = (bf16[256,512]{1,0:T(8,128)(2,1)S(1)}, bf16[256,512]{1,0:T(8,128)(2,1)}, u32[]{:S(2)}) copy-start(bf16[256,512]{1,0:T(8,128)(2,1)} %param.7) | copy-start | bytes 786436

commit v3 on v2

--- a/solution.py
+++ b/solution.py
@@ -163,7 +163,7 @@
 F32 = jnp.float32
 BF16 = jnp.bfloat16
 MESH = pl.DeviceIdType.MESH
-N_SEMS = 38
+N_SEMS = 72
 
 
 def rows_of(index, size):
@@ -175,7 +175,7 @@
     rows_ref, w_ref,
     out_ref, gsig_ref, gq_ref, gk_ref, gv_ref, go_ref,
     weights, sig_all, up_all, normed, qkv, gctx, ctx, grads3,
-    partial, landed, summed, landed_z, final,
+    partial, relay_in, relay_out, landed, summed, landed_z, final,
     out_send, out_recv, gn_send, gn_recv, send_sems, recv_sems,
 ):
     block, frames = w_ref.shape[0] // 4, rows_ref.shape[0] // 2
@@ -187,7 +187,10 @@
     piece = block // n_dp
     scale = HSIZE ** (-0.5)
 
-    def copy(src, dst, sem, axis, to):
+    slots = {}
+
+    def copy(src, dst, name, axis, to):
+        sem = slots.setdefault(name, len(slots))
         return pltpu.make_async_remote_copy(
             src_ref=src, dst_ref=dst, send_sem=send_sems.at[sem], recv_sem=recv_sems.at[sem],
             device_id={axis: to}, device_id_type=MESH,
@@ -199,6 +202,10 @@
     def back(index, step, size):
         return lax.rem(index + size - step, size)
 
+    x_peer = dp + 1 - 2 * lax.rem(dp, 2)
+    y_peer = lax.rem(dp + 2, n_dp)
+    diagonal = n_dp - 1 - dp
+    sibling = 1 - core
     barrier = pltpu.get_barrier_semaphore()
     for step in range(1, n_dp):
         pl.semaphore_signal(barrier, inc=1, device_id={"dp": forth(dp, step, n_dp)}, device_id_type=MESH)
@@ -219,39 +226,54 @@
         one.start()
         sends.append(one)
 
-    def arrived(dst, sem):
-        copy(dst, dst, sem, "seq", 1 - core).wait_recv()
+    def arrived(dst, name):
+        copy(dst, dst, name, "seq", sibling).wait_recv()
+
+    low, high = slice(0, piece // 2), slice(piece // 2, piece)
+    half_piece = piece // 2
 
     def weight_rows(shard, quarter):
         return weights.at[pl.ds(pl.multiple_of(shard * block + quarter * piece, piece), piece)]
 
+    def weight_half(shard, quarter, side):
+        first = shard * block + quarter * piece + side * half_piece
+        return weights.at[pl.ds(pl.multiple_of(first, half_piece), half_piece)]
+
     mine = weight_rows(z, dp)
     for step in (1, 2, 3):
-        start(mine, mine, step - 1, "fsdp", forth(z, step, n_z))
+        start(mine, mine, ("wz", step), "fsdp", forth(z, step, n_z))
     own_frames = rows_of(core, frames)
     far_frames = rows_of(1 - core, frames)
-    start(sig_ref, sig_all.at[own_frames], 12, "seq", 1 - core)
-    start(up_ref, up_all.at[own_frames], 13, "seq", 1 - core)
+    start(sig_ref, sig_all.at[own_frames], "sig", "seq", 1 - core)
+    start(up_ref, up_all.at[own_frames], "up", "seq", 1 - core)
     normed_f, inverse = normalize(sig_ref[...])
     normed[own_frames, :] = normed_f.astype(BF16)
     up_all[own_frames, :] = up_ref[...]
-    arrived(sig_all.at[far_frames], 12)
+    arrived(sig_all.at[far_frames], "sig")
     far_normed, _ = normalize(sig_all[far_frames, :])
     normed[far_frames, :] = far_normed.astype(BF16)
-    arrived(up_all.at[far_frames], 13)
-
-    for step in (1, 2, 3):
+    arrived(up_all.at[far_frames], "up")
+
+    def spread(step):
+        held = weight_rows(back(z, step, n_z), dp)
+        arrived(held, ("wz", step))
+        start(held, held, ("wx", step), "dp", x_peer)
+        start(held, held, ("wy", step), "dp", y_peer)
+
+    def pass_on(step):
         source = back(z, step, n_z)
-        held = weight_rows(source, dp)
-        arrived(held, step - 1)
-        for peer in (1, 2, 3):
-            start(held, held, 3 + (step - 1) * 3 + peer - 1, "dp", forth(dp, peer, n_dp))
-
-    for step in (0, 1, 2, 3):
+        arrived(weight_rows(source, x_peer), ("wx", step))
+        held = weight_half(source, x_peer, 0)
+        start(held, held, ("wfy", step), "dp", y_peer)
+        arrived(weight_rows(source, y_peer), ("wy", step))
+        held = weight_half(source, y_peer, 1)
+        start(held, held, ("wfx", step), "dp", x_peer)
+
+    def project(step):
         source = back(z, step, n_z)
         if step:
-            for peer in (1, 2, 3):
-                arrived(weight_rows(source, back(dp, peer, n_dp)), 3 + (step - 1) * 3 + peer - 1)
+            arrived(weight_half(source, diagonal, 0), ("wfy", step))
+            arrived(weight_half(source, diagonal, 1), ("wfx", step))
         rows = rows_of(source, block)
         first = jnp.dot(normed[:, rows], weights[rows, : 3 * half], preferred_element_type=F32)
         second = jnp.dot(up_all[:, rows], weights[rows, 3 * half :], preferred_element_type=F32)
@@ -260,6 +282,14 @@
             second = gctx[...] + second
         qkv[...] = first
         gctx[...] = second
+
+    for step in (1, 2, 3):
+        spread(step)
+    project(0)
+    for step in (1, 2, 3):
+        pass_on(step)
+    for step in (1, 2, 3):
+        project(step)
 
     for head in range(half // HSIZE):
         cols = slice(head * HSIZE, (head + 1) * HSIZE)
@@ -284,37 +314,63 @@
         ).astype(BF16)
 
     order = (2, 1, 3, 0)
+
+    def half_rows(step, quarter, side):
+        first = quarter * piece + side * half_piece
+        return partial.at[step, pl.ds(pl.multiple_of(first, half_piece), half_piece)]
+
     for step in order:
         cols = rows_of(forth(z, step, n_z), block)
         partial[step, :, : 3 * half] = dot_across(normed[:, cols], grads3[...]).astype(BF16)
         partial[step, :, 3 * half :] = dot_across(up_all[:, cols], ctx[...]).astype(BF16)
-        for peer in (1, 2, 3):
-            to = forth(dp, peer, n_dp)
+        for side, peer, name in ((0, x_peer, "x"), (1, y_peer, "y")):
             start(
-                partial.at[step, rows_of(to, piece)], landed.at[step, peer - 1],
-                14 + step * 3 + peer - 1, "dp", to,
+                half_rows(step, diagonal, side), relay_in.at[step, side],
+                ("relay" + name, step), "dp", peer,
             )
-
+            start(
+                half_rows(step, peer, side), landed.at[step, side, 0],
+                ("near" + name, step), "dp", peer,
+            )
+
+    def relay(step):
+        for side, peer, name in ((0, y_peer, "x"), (1, x_peer, "y")):
+            arrived(relay_in.at[step, side], ("relay" + name, step))
+            first = peer * piece + side * half_piece
+            rows = pl.ds(pl.multiple_of(first, half_piece), half_piece)
+            both = partial[step, rows, :].astype(F32) + relay_in[step, side].astype(F32)
+            relay_out[step, side] = both.astype(BF16)
+            start(
+                relay_out.at[step, side], landed.at[step, side, 1],
+                ("far" + name, step), "dp", peer,
+            )
+
+    relay(order[0])
+    relay(order[1])
     out_send[...] = dot_against(ctx[far_frames, :], weights[:, 3 * half :])
-    start(out_send, out_recv, 26, "seq", 1 - core)
+    start(out_send, out_recv, "out", "seq", 1 - core)
+    relay(order[2])
     gn_send[...] = dot_against(grads3[far_frames, :], weights[:, : 3 * half])
-    start(gn_send, gn_recv, 27, "seq", 1 - core)
+    start(gn_send, gn_recv, "gn", "seq", 1 - core)
+    relay(order[3])
     out_own = dot_against(ctx[own_frames, :], weights[:, 3 * half :])
-    arrived(out_recv, 26)
+    arrived(out_recv, "out")
     out_ref[...] = (sig_ref[...].astype(F32) + (out_own + out_recv[...])).astype(BF16)
 
     for step in order:
-        for peer in (1, 2, 3):
-            arrived(landed.at[step, peer - 1], 14 + step * 3 + peer - 1)
-        total = partial[step, rows_of(dp, piece), :].astype(F32)
-        for peer in (1, 2, 3):
-            total = total + landed[step, peer - 1].astype(F32)
-        summed[step] = total.astype(BF16)
+        for side, name in ((0, "x"), (1, "y")):
+            arrived(landed.at[step, side, 0], ("near" + name, step))
+            arrived(landed.at[step, side, 1], ("far" + name, step))
+            first = dp * piece + side * half_piece
+            rows = pl.ds(pl.multiple_of(first, half_piece), half_piece)
+            total = partial[step, rows, :].astype(F32)
+            total = total + landed[step, side, 0].astype(F32) + landed[step, side, 1].astype(F32)
+            summed[step, (low, high)[side], :] = total.astype(BF16)
         if step:
-            start(summed.at[step], landed_z.at[step - 1], 28 + step - 1, "fsdp", forth(z, step, n_z))
+            start(summed.at[step], landed_z.at[step - 1], ("sz", step), "fsdp", forth(z, step, n_z))
 
     gn_own = dot_against(grads3[own_frames, :], weights[:, : 3 * half])
-    arrived(gn_recv, 27)
+    arrived(gn_recv, "gn")
     grad_normed = gn_own + gn_recv[...]
     normed_f, inverse = normalize(sig_ref[...])
     grad_mean = jnp.mean(grad_normed, axis=-1, keepdims=True)
@@ -325,20 +381,40 @@
 
     total = summed[0].astype(F32)
     for step in (1, 2, 3):
-        arrived(landed_z.at[step - 1], 28 + step - 1)
+        arrived(landed_z.at[step - 1], ("sz", step))
         total = total + landed_z[step - 1].astype(F32)
     own_piece = rows_of(dp, piece)
     final[core, own_piece, :] = total.astype(BF16)
-    place = final.at[core, own_piece]
-    for peer in (1, 2, 3):
-        start(place, place, 31 + peer - 1, "dp", forth(dp, peer, n_dp))
-    start(place, place, 34, "seq", 1 - core)
-    for peer in (1, 2, 3):
-        place = final.at[core, rows_of(back(dp, peer, n_dp), piece)]
-        arrived(place, 31 + peer - 1)
-        start(place, place, 34 + peer, "seq", 1 - core)
-    for peer in (0, 1, 2, 3):
-        arrived(final.at[1 - core, rows_of(back(dp, peer, n_dp), piece)], 34 + peer)
+    def final_half(side_core, quarter, side):
+        first = quarter * piece + side * half_piece
+        return final.at[side_core, pl.ds(pl.multiple_of(first, half_piece), half_piece)]
+
+    def final_rows(side_core, quarter):
+        return final.at[side_core, rows_of(quarter, piece)]
+
+    place = final_rows(core, dp)
+    start(place, place, "fx", "dp", x_peer)
+    start(place, place, "fy", "dp", y_peer)
+    start(place, place, "fs0", "seq", sibling)
+    place = final_rows(core, x_peer)
+    arrived(place, "fx")
+    part = final_half(core, x_peer, 0)
+    start(part, part, "ffy", "dp", y_peer)
+    start(place, place, "fsx", "seq", sibling)
+    place = final_rows(core, y_peer)
+    arrived(place, "fy")
+    part = final_half(core, y_peer, 1)
+    start(part, part, "ffx", "dp", x_peer)
+    start(place, place, "fsy", "seq", sibling)
+    for side, name in ((0, "y"), (1, "x")):
+        part = final_half(core, diagonal, side)
+        arrived(part, "ff" + name)
+        start(part, part, "ffs" + name, "seq", sibling)
+    arrived(final_rows(sibling, dp), "fs0")
+    arrived(final_rows(sibling, x_peer), "fsx")
+    arrived(final_rows(sibling, y_peer), "fsy")
+    arrived(final_half(sibling, diagonal, 0), "ffsy")
+    arrived(final_half(sibling, diagonal, 1), "ffsx")
 
     factor = token_count ** (-0.5)
     for at, ref in enumerate((gq_ref, gk_ref, gv_ref, go_ref)):
@@ -379,7 +455,9 @@
             pltpu.VMEM((both, half), BF16),
             pltpu.VMEM((both, 3 * half), BF16),
             pltpu.VMEM((n_z, block, 4 * half), BF16),
-            pltpu.VMEM((n_z, n_dp - 1, piece, 4 * half), BF16),
+            pltpu.VMEM((n_z, 2, piece // 2, 4 * half), BF16),
+            pltpu.VMEM((n_z, 2, piece // 2, 4 * half), BF16),
+            pltpu.VMEM((n_z, 2, 2, piece // 2, 4 * half), BF16),
             pltpu.VMEM((n_z, piece, 4 * half), BF16),
             pltpu.VMEM((n_z - 1, piece, 4 * half), BF16),
             pltpu.VMEM((2, block, 4 * half), BF16),

time: 71.1 us -> 70.5 us (level)
  no operation moved by 1% of the time
where the time goes in v3:
time: 70.5 us; the launch traced here: 70.3 us
  Pallas kernels  63.7 us (90%)
  local copies, waits for them, and re-layouts  4.73 us (7%)
  other arithmetic  1.21 us (2%)
    pallas_call x1, Pallas kernels, fused_body(): pl.pallas_call(kernel, out_shape=[rows_shape, rows_shape] + [grad_shape]...  63.7 us
    unnamed x14, local copies, waits for them, and re-layouts  4.73 us

profile of v3, /device:TPU:1, one launch (start us, length us, event | category | flops | bytes accessed | tf_op | source)
XLA Modules:
  0.0 70.3 jit_solution(10337790855072376143)
XLA Ops:
  0.6 0.0 copy-start
  0.6 0.0 copy-start.1
  0.7 0.0 copy-start.2
  0.7 0.0 copy-start.3
  0.7 1.1 %pad_maximum_fusion.1.refs_0_ = bf16[256,1024]{1,0:T(8,128)(2,1)S(1)} fusion(bf16[128,1024]{1,0:T(8,128)(2,1)} %bitcast.6, bf16[128,1024]{1,0:T(8,128)(2,1)} %bitcast.7), kind=kLoop, calls=%fused_computation.1 | loop fusion | flops 1048576 | bytes 1048576 | tf_op jit(solution)/shard_map/concatenate | solution.py:475
  1.8 0.0 copy-done
  1.8 0.0 copy-done.1
  1.8 0.1 copy-done.2
  1.9 0.1 copy-done.3
  2.0 0.1 pad_maximum_fusion.refs_1_
  2.1 63.7 %shard_map.109 = (bf16[128,1024]{1,0:T(8,128)(2,1)S(1)}, bf16[128,1024]{1,0:T(8,128)(2,1)S(1)}, f32[256,512]{1,0:T(8,128)S(1)}, f32[256,512]{1,0:T(8,128)S(1)}, ...) custom-call(bf16[256,1024]{1,0:T(8,128)(2,1)S(1)} %pad_maximum_fusion.1.refs_0_, bf16[1024,512]{1,0:T(8,128)(2,1)S(1)} %pad_maximum_fusion.refs_1_), custom_call_target="tpu_custom_call" | custom-call | tf_op jit(solution)/shard_map/pallas_call | solution.py:443
  65.8 0.7 %copy.18 = bf16[1,128,1024]{2,1,0:T(8,128)(2,1)} copy(bf16[1,128,1024]{2,1,0:T(8,128)(2,1)S(1)} %bitcast.5) | data formatting | bytes 524288
  66.5 0.7 copy.19
  67.2 0.8 %copy.20 = f32[256,512]{1,0:T(8,128)} copy(f32[256,512]{1,0:T(8,128)S(1)} %get-tuple-element.26) | data formatting | bytes 1048576
  68.0 0.8 %copy.21 = f32[256,512]{1,0:T(8,128)} copy(f32[256,512]{1,0:T(8,128)S(1)} %get-tuple-element.27) | data formatting | bytes 1048576
  68.8 0.8 %copy.22 = f32[256,512]{1,0:T(8,128)} copy(f32[256,512]{1,0:T(8,128)S(1)} %get-tuple-element.28) | data formatting | bytes 1048576
  69.6 0.8 %copy.23 = f32[256,512]{1,0:T(8,128)} copy(f32[256,512]{1,0:T(8,128)S(1)} %get-tuple-element.29) | data formatting | bytes 1048576
Async XLA Ops:
  0.6 1.2 %copy-start = (bf16[256,512]{1,0:T(8,128)(2,1)S(1)}, bf16[256,512]{1,0:T(8,128)(2,1)}, u32[]{:S(2)}) copy-start(bf16[256,512]{1,0:T(8,128)(2,1)} %param.10) | copy-start | bytes 786436
  0.6 1.2 %copy-start.1 = (bf16[256,512]{1,0:T(8,128)(2,1)S(1)}, bf16[256,512]{1,0:T(8,128)(2,1)}, u32[]{:S(2)}) copy-start(bf16[256,512]{1,0:T(8,128)(2,1)} %param.9) | copy-start | bytes 786436
  0.7 1.2 %copy-start.2 = (bf16[256,512]{1,0:T(8,128)(2,1)S(1)}, bf16[256,512]{1,0:T(8,128)(2,1)}, u32[]{:S(2)}) copy-start(bf16[256,512]{1,0:T(8,128)(2,1)} %param.8) | copy-start | bytes 786436
  0.7 1.3 %copy-start.3 = (bf16[256,512]{1,0:T(8,128)(2,1)S(1)}, bf16[256,512]{1,0:T(8,128)(2,1)}, u32[]{:S(2)}) copy-start(bf16[256,512]{1,0:T(8,128)(2,1)} %param.7) | copy-start | bytes 786436
